TPU v7x, 32 devices: a whole 2x2x4 slice. The times are simulated.
32 devices in a mesh: dp: 2 (over y), expert: 16 (over z, x, core).
Axes of the slice: x: 2, y: 2, z: 4, core: 2. Of those that a mesh axis runs over, the one named last changes fastest.
Arguments:
- grad_out: bfloat16 [8192, 4096], P('expert', 'dp'), may hold values from -30 to 30
- hidden: bfloat16 [8192, 2, 1024], P('expert', None, 'dp'), may hold values from -24 to 24
- gate_prob: float32 [8192, 2], P('expert'), may hold values from 0.05 to 1
- expert_ids: int32 [8192, 2], P('expert'), may hold values from 0 to 15, all different within a row; in each aligned block of 512 rows (0 to 511, 512 to 1023, ...) at most 80 rows name the same one
- weights: bfloat16 [16, 1024, 4096], P('expert', None, 'dp'), may hold values from -0.1875 to 0.1875
Outputs:
- hidden_grad: bfloat16 [8192, 2, 1024], P('expert', None, 'dp')
- update: float32 [16, 1024, 4096], P('expert', None, 'dp')
Inputs may be any that keep to these rules, and one draw needn't show every extreme that they name: `expert_ids`: among the 512 tokens of one index of expert, no expert is named by more than 80 choices, a bound that some block reaches; the 2 experts of a token differ.
All inputs are finite; a program needn't handle non-finite values.
Results may differ from a plain program's by a relative error of at most 0.019.
Values may be sent and summed in bfloat16 or wider, within the bound.
A program may use at most 64 MiB of HBM per device.

v0:
```python
import jax
import jax.numpy as jnp
from jax import lax
from jax.sharding import PartitionSpec as P

D = 4096


def slot_numbers(route_ids, capacity, expert_count):
    flat_ids = route_ids.reshape(-1)
    one_hot = (flat_ids[:, None] == jnp.arange(expert_count, dtype=jnp.int32)[None, :]).astype(
        jnp.int32
    )
    before = jnp.cumsum(one_hot, axis=0) - one_hot
    rank_in = jnp.sum(before * one_hot, axis=1)
    return flat_ids * capacity + rank_in


def gram_sum(matrix_part):
    partial_gram = jnp.dot(matrix_part, matrix_part.T, preferred_element_type=jnp.float32)
    return lax.psum(partial_gram.astype(jnp.bfloat16), "dp").astype(jnp.float32)


def place_slots(slot_index, values, slot_count):
    empty_rows = jnp.zeros((slot_count,) + values.shape[1:], values.dtype)
    return empty_rows.at[slot_index].set(values)


def per_device(grad_out, hidden, gate_prob, expert_ids, weights):
    tokens, width_part = grad_out.shape
    top_count = expert_ids.shape[1]
    experts = lax.axis_size("expert")
    capacity = 5 * tokens * top_count // (4 * experts)
    total_slots = experts * capacity
    pair_count = tokens * top_count
    slot_index = slot_numbers(expert_ids, capacity, experts)
    token_of = jnp.arange(pair_count, dtype=jnp.int32) // top_count
    send_grad = place_slots(slot_index, grad_out[token_of], total_slots).reshape(
        experts, capacity, width_part
    )
    scaled_part = (gate_prob[:, :, None] * hidden.astype(jnp.float32)).astype(jnp.bfloat16)
    whole_scaled = lax.all_gather(scaled_part, "dp", axis=2, tiled=True)
    send_scaled = place_slots(
        slot_index, whole_scaled.reshape(pair_count, -1), total_slots
    ).reshape(experts, capacity, -1)
    got_grad, got_scaled = (
        lax.all_to_all(send_grad, "expert", split_axis=0, concat_axis=0, tiled=True),
        lax.all_to_all(send_scaled, "expert", split_axis=0, concat_axis=0, tiled=True),
    )
    got_grad = got_grad.reshape(total_slots, width_part)
    got_scaled = got_scaled.reshape(total_slots, -1)
    weight_part = weights[0]
    gradient = lax.dot_general(
        got_scaled, got_grad, (((0,), (0,)), ((), ())), preferred_element_type=jnp.float32
    )
    back_term = lax.dot_general(
        got_grad, weight_part, (((1,), (1,)), ((), ())), preferred_element_type=jnp.float32
    )
    flat_prob = gate_prob.reshape(-1)
    summed = lax.psum_scatter(
        back_term.astype(jnp.bfloat16), "dp", scatter_dimension=1, tiled=True
    ).astype(jnp.float32)
    returned = lax.all_to_all(
        summed.reshape(experts, capacity, -1).astype(jnp.bfloat16),
        "expert",
        split_axis=0,
        concat_axis=0,
        tiled=True,
    ).astype(jnp.float32)
    picked = returned.reshape(total_slots, -1)[slot_index]
    hidden_grad = (flat_prob[:, None] * picked).astype(jnp.bfloat16).reshape(tokens, top_count, -1)
    grad_bf16 = gradient.astype(jnp.bfloat16)
    gram_first = gram_sum(grad_bf16)
    norm_sq = jnp.sqrt(jnp.sum(gram_first * gram_first)) + 1e-06
    current = (grad_bf16.astype(jnp.float32) * lax.rsqrt(norm_sq)).astype(jnp.bfloat16)
    gram_now = (gram_first / norm_sq).astype(jnp.bfloat16)
    following = current.astype(jnp.float32)
    for sweep_number in range(2):
        if sweep_number > 0:
            gram_now = gram_sum(current).astype(jnp.bfloat16)
        following = 1.5 * current.astype(jnp.float32) - 0.5 * jnp.dot(
            gram_now, current, preferred_element_type=jnp.float32
        )
        current = following.astype(jnp.bfloat16)
    update = following * D**0.5
    return (hidden_grad, update[None])


def solution(mesh):
    in_specs = (
        P("expert", "dp"),
        P("expert", None, "dp"),
        P("expert", None),
        P("expert", None),
        P("expert", None, "dp"),
    )
    out_specs = (P("expert", None, "dp"), P("expert", None, "dp"))
    return jax.shard_map(
        per_device, mesh=mesh, in_specs=in_specs, out_specs=out_specs, check_vma=False
    )
```

profile of v0, /device:TPU:11, one launch (start us, length us, event | category | flops | bytes accessed | tf_op | source)
XLA Modules:
  0.0 554.2 jit_solution(17177138746573710264)
XLA Ops:
  7.2 0.0 copy-start
  7.2 0.0 reduce-scatter.2.cloned.1.call-start
  7.2 0.8 broadcast_multiply_fusion
  8.1 0.8 copy.12
  8.9 0.2 eq.29
  9.1 0.2 eq.25
  9.3 0.1 copy.11
  9.4 0.2 mul.64
  9.6 4.5 reduce-window.6
  14.1 0.1 slice.12
  14.2 0.1 copy.14
  14.4 0.1 copy.15
  14.4 0.1 broadcast_add_fusion
  14.6 23.4 %scatter_custom_fusion = bf16[1280,2048]{1,0:T(8,128)(2,1)} fusion(s32[1024]{0:T(1024)S(1)} %bitcast.54, bf16[512,2048]{1,0:T(8,128)(2,1)S(1)} %copy-done, s32[1024]{0:T(1024)S(1)} %broadcast_clamp_fusion.1, bf16[]{:T(256)} %constant.13.clone.1), kind=kCustom, calls=%fused_computation.14 | custom fusion | bytes 5242882 | tf_op jit(solution)/shard_map/scatter | solution.py:26
  38.0 0.0 copy-start.4
  38.0 121.6 %all_to_all.15 = bf16[16,80,2048]{2,1,0:T(8,128)(2,1)} all-to-all(bf16[16,80,2048]{2,1,0:T(8,128)(2,1)} %bitcast.48), channel_id=1, replica_groups=mesh['dp'=2,'expert'=16] {'expert'}, dimensions={0} | all-to-all | bytes 10485760 | tf_op jit(solution)/shard_map/all_to_all | solution.py:47
  159.7 9.5 %fusion.7 = bf16[1280,1024]{1,0:T(8,128)(2,1)} fusion(bf16[1280,2048]{1,0:T(8,128)(2,1)} %bitcast.6, bf16[1,1024,2048]{2,1,0:T(8,128)(2,1)S(1)} %copy-done.4), kind=kOutput, calls=%fused_computation.17 | convolution fusion | flops 5370019840 | bytes 12058624 | tf_op jit(solution)/shard_map/dot_general | solution.py:56
  169.2 0.0 reduce-scatter.2.cloned.1.call-update
  169.2 37.7 %reduce-scatter.2.cloned.1.call-done = bf16[1280,512]{1,0:T(8,128)(2,1)} async-done(((bf16[1280,1024]{1,0:T(8,128)(2,1)}), bf16[1280,512]{1,0:T(8,128)(2,1)}) %reduce-scatter.2.cloned.1.call-update) | async-done | bytes 1310736 | tf_op jit(solution)/shard_map/reduce_scatter | solution.py:60
  207.0 6.4 %all-to-all-start.1 = ((bf16[16,80,512]{2,1,0:T(8,128)(2,1)}), bf16[16,80,512]{2,1,0:T(8,128)(2,1)}, u32[]{:S(2)}, u32[]{:S(2)}) async-start(bf16[16,80,512]{2,1,0:T(8,128)(2,1)} %bitcast.50), calls=%async_computation.2 | async-start | bytes 2621440 | tf_op jit(solution)/shard_map/all_to_all | solution.py:63
  213.3 0.0 all-gather.2.cloned.1.call-start
  213.4 0.1 copy.10
  213.5 30.4 %all-to-all-done.1 = bf16[16,80,512]{2,1,0:T(8,128)(2,1)} async-done(((bf16[16,80,512]{2,1,0:T(8,128)(2,1)}), bf16[16,80,512]{2,1,0:T(8,128)(2,1)}, u32[]{:S(2)}, u32[]{:S(2)}) %all-to-all-start.1) | async-done | bytes 1310752 | tf_op jit(solution)/shard_map/all_to_all | solution.py:63
  244.0 1.7 bitcast_convert_fusion.1
  245.7 4.9 gather_fusion
  250.5 2.6 gather.10
  253.1 0.0 copy-done.2
  253.1 2.7 multiply_convert_fusion.2
  255.8 0.0 all-gather.2.cloned.1.call-update
  255.8 0.0 all-reduce.3.cloned.1.call-start
  255.9 31.7 %all-gather.2.cloned.1.call-done = bf16[512,2,1024]{2,1,0:T(2,128)(2,1)} async-done(((bf16[512,2,512]{2,1,0:T(2,128)(2,1)}), bf16[512,2,1024]{2,1,0:T(2,128)(2,1)}) %all-gather.2.cloned.1.call-update) | async-done | bytes 2097168 | tf_op jit(solution)/shard_map/all_gather | solution.py:42
  287.6 4.1 reshape.160
  291.7 6.8 %scatter_custom_fusion.1 = bf16[1280,1024]{1,0:T(8,128)(2,1)S(1)} fusion(s32[1024]{0:T(1024)S(1)} %bitcast.56, bf16[1024,1024]{1,0:T(8,128)(2,1)} %reshape.160, bf16[]{:T(256)} %constant.13.clone.1), kind=kCustom, calls=%fused_computation.25 | custom fusion | bytes 2621952 | tf_op jit(solution)/shard_map/scatter | solution.py:26
  298.5 75.3 %all_to_all.16 = bf16[16,80,1024]{2,1,0:T(8,128)(2,1)S(1)} all-to-all(bf16[16,80,1024]{2,1,0:T(8,128)(2,1)S(1)} %bitcast.49), channel_id=1, replica_groups=mesh['dp'=2,'expert'=16] {'expert'}, dimensions={0} | all-to-all | bytes 5242880 | tf_op jit(solution)/shard_map/all_to_all | solution.py:48
  373.7 8.4 %bitcast_convert_fusion = bf16[1024,2048]{1,0:T(8,128)(2,1)S(1)} fusion(bf16[16,80,1024]{2,1,0:T(8,128)(2,1)S(1)} %all_to_all.16, bf16[16,80,2048]{2,1,0:T(8,128)(2,1)} %all_to_all.15), kind=kOutput, calls=%fused_computation.4 | convolution fusion | flops 5370806272 | bytes 12058624 | tf_op jit(solution)/shard_map/dot_general | solution.py:53
  382.2 0.0 copy-start.5
  382.2 2.0 copy-done.5
  384.2 5.8 %convolution_convert_fusion.1 = bf16[1024,1024]{1,0:T(8,128)(2,1)} fusion(bf16[1024,2048]{1,0:T(8,128)(2,1)S(1)} %bitcast_convert_fusion), kind=kOutput, calls=%fused_computation.23 | convolution fusion | flops 4296015872 | bytes 6291456 | tf_op jit(solution)/shard_map/dot_general | solution.py:20
  389.9 0.0 all-reduce.3.cloned.1.call-update
  390.0 0.0 all-reduce.5.cloned.1.call-start
  390.0 61.8 %all-reduce.3.cloned.1.call-done = bf16[1024,1024]{1,0:T(8,128)(2,1)} async-done(((bf16[1024,1024]{1,0:T(8,128)(2,1)}), bf16[1024,1024]{1,0:T(8,128)(2,1)}) %all-reduce.3.cloned.1.call-update) | async-done | bytes 2097168 | tf_op jit(solution)/shard_map/psum | solution.py:21
  451.8 3.3 fusion
  455.8 8.8 %subtract_convert_fusion = bf16[1024,2048]{1,0:T(8,128)(2,1)S(1)} fusion(bf16[1024,2048]{1,0:T(8,128)(2,1)} %copy-done.5, f32[]{:T(128)S(6)} %rsqrt.3, bf16[1024,1024]{1,0:T(8,128)(2,1)} %all-reduce.3.cloned.1.call-done, f32[]{:T(128)S(6)} %add.56), kind=kOutput, calls=%fused_computation.6 | convolution fusion | flops 4321181696 | bytes 10485768 | tf_op jit(solution)/shard_map/dot_general | solution.py:81
  464.6 1.9 copy-done.6
  466.5 5.7 %convolution_convert_fusion = bf16[1024,1024]{1,0:T(8,128)(2,1)} fusion(bf16[1024,2048]{1,0:T(8,128)(2,1)S(1)} %subtract_convert_fusion), kind=kOutput, calls=%fused_computation.22 | convolution fusion | flops 4296015872 | bytes 6291456 | tf_op jit(solution)/shard_map/dot_general | solution.py:20
  472.3 0.0 all-reduce.5.cloned.1.call-update
  472.3 63.1 %all-reduce.5.cloned.1.call-done = bf16[1024,1024]{1,0:T(8,128)(2,1)} async-done(((bf16[1024,1024]{1,0:T(8,128)(2,1)}), bf16[1024,1024]{1,0:T(8,128)(2,1)}) %all-reduce.5.cloned.1.call-update) | async-done | bytes 2097168 | tf_op jit(solution)/shard_map/psum | solution.py:21
  535.3 12.2 %multiply_bitcast_fusion = f32[1,1024,2048]{2,1,0:T(8,128)} fusion(bf16[1024,2048]{1,0:T(8,128)(2,1)} %copy-done.6, bf16[1024,1024]{1,0:T(8,128)(2,1)} %all-reduce.5.cloned.1.call-done), kind=kOutput, calls=%fused_computation.5 | convolution fusion | flops 4305453056 | bytes 14680064 | tf_op jit(solution)/shard_map/dot_general | solution.py:81
  (16 shorter events, 0.1 us)
Async XLA Ops:
  7.2 7.4 %copy-start = (bf16[512,2048]{1,0:T(8,128)(2,1)S(1)}, bf16[512,2048]{1,0:T(8,128)(2,1)}, u32[]{:S(2)}) copy-start(bf16[512,2048]{1,0:T(8,128)(2,1)} %param.5) | copy-start | bytes 6291460
  7.2 199.8 %reduce-scatter.2.cloned.1.call-start = ((), (), s32[]{:S(2)}) async-start(), calls=%async_computation.4 | async-start | bytes 3932160 | tf_op jit(solution)/shard_map/reduce_scatter | solution.py:60
  38.0 121.7 %copy-start.4 = (bf16[1,1024,2048]{2,1,0:T(8,128)(2,1)S(1)}, bf16[1,1024,2048]{2,1,0:T(8,128)(2,1)}, u32[]{:S(2)}) copy-start(bf16[1,1024,2048]{2,1,0:T(8,128)(2,1)} %param.9) | copy-start | bytes 12582916
  169.2 44.2 %copy-start.3 = (f32[512,2]{0,1:T(2,128)S(1)}, f32[512,2]{0,1:T(2,128)}, u32[]{:S(2)}) copy-start(f32[512,2]{0,1:T(2,128)} %param.7) | copy-start | bytes 12292
  207.0 37.0 %all-to-all-start.1 = ((bf16[16,80,512]{2,1,0:T(8,128)(2,1)}), bf16[16,80,512]{2,1,0:T(8,128)(2,1)}, u32[]{:S(2)}, u32[]{:S(2)}) async-start(bf16[16,80,512]{2,1,0:T(8,128)(2,1)} %bitcast.50), calls=%async_computation.2 | async-start | bytes 2621440 | tf_op jit(solution)/shard_map/all_to_all | solution.py:63
  213.3 74.2 %all-gather.2.cloned.1.call-start = ((), (), s32[]{:S(2)}) async-start(), calls=%async_computation.5 | async-start | bytes 3145728 | tf_op jit(solution)/shard_map/all_gather | solution.py:42
  250.5 2.6 copy-start.2
  255.8 196.0 %all-reduce.3.cloned.1.call-start = ((), (), s32[]{:S(2)}) async-start(), calls=%async_computation.6 | async-start | bytes 4194304 | tf_op jit(solution)/shard_map/psum | solution.py:21
  382.2 2.0 copy-start.5
  390.0 145.4 %all-reduce.5.cloned.1.call-start = ((), (), s32[]{:S(2)}) async-start(), calls=%async_computation.7 | async-start | bytes 4194304 | tf_op jit(solution)/shard_map/psum | solution.py:21
  464.6 1.9 copy-start.6
  535.3 12.2 %copy-start.1 = (bf16[512,2048]{1,0:T(8,128)(2,1)S(1)}, bf16[512,2048]{1,0:T(8,128)(2,1)}, u32[]{:S(2)}) copy-start(bf16[512,2048]{1,0:T(8,128)(2,1)} %param.5) | copy-start | bytes 6291460
Sparse Core Ops, SparseCore 0:
  169.4 37.5 reduce-scatter.1
  255.9 31.5 all-gather.1
  390.1 61.6 all-reduce.2
  472.4 62.8 all-reduce.4
where the time goes:
time: 561 us; the launch traced here: 554 us
  waiting for transfers between devices  225 us (40%)
  blocking collectives  197 us (35%)
  matrix products  50.4 us (9%)
  local copies, waits for them, and re-layouts  47.6 us (8%)
  between operations  14.9 us (3%)
  other arithmetic  13.1 us (2%)
  starting transfers between devices  6.53 us (1%)
    psum x2, waiting for transfers between devices, gram_sum(): return lax.psum(partial_gram.astype(jnp.bfloat16), 'dp').astype(jnp.float32)  125 us
    all_to_all x1, blocking collectives, per_device(): lax.all_to_all(send_grad, 'expert', split_axis=0, concat_axis=0, tiled=True)  122 us
    all_to_all x1, blocking collectives, per_device(): lax.all_to_all(send_scaled, 'expert', split_axis=0, concat_axis=0, tiled=...  75.3 us
    reduce_scatter x1, waiting for transfers between devices, per_device(): lax.psum_scatter(back_term.astype(jnp.bfloat16), 'dp', scatter_dimension=...  37.7 us
    all_gather x1, waiting for transfers between devices, per_device(): whole_scaled = lax.all_gather(scaled_part, 'dp', axis=2, tiled=True)  31.7 us
    all_to_all x1, waiting for transfers between devices, per_device(): lax.all_to_all(summed.reshape(experts, capacity, -1).astype(jnp.bfloat16)...  30.4 us
    scatter x2, local copies, waits for them, and re-layouts, place_slots(): return empty_rows.at[slot_index].set(values)  30.2 us
    dot_general x2, matrix products, per_device(): jnp.dot(gram_now, current, preferred_element_type=jnp.float32)  21 us
  transfers between devices with their start and end apart: 5, of which 5 were waited for; matrix products, arithmetic and copies ran while one was open for 0% of the time, Pallas kernels for 0%

commit v1 on v0

v1 whole, which is shorter than its diff:
```python
import functools

import jax
import jax.numpy as jnp
from jax import lax
from jax.experimental import pallas as pl
from jax.experimental.pallas import tpu as pltpu
from jax.sharding import PartitionSpec as P

D = 4096
MESH = pl.DeviceIdType.MESH
BF16 = jnp.bfloat16
F32 = jnp.float32
GROUPS = 4


def dot(a, b, dims=((1,), (0,))):
    return lax.dot_general(a, b, (dims, ((), ())), preferred_element_type=F32)


def kernel(
    n, ndp, cap,
    ids_ref, grad_ref, scaled_ref, weight_ref,
    g_ref, p_ref, c_ref, picked_ref,
    rank0, rank1, select, send_grad, got_grad, send_scaled, got_scaled, scaled_t,
    back_part, back_got, summed, returned,
    gram_part, gram_got, gram_sum, a_ref, a2_ref, w_ref,
    grad_s, grad_r, sc_s, sc_r, ret_s, ret_r, ysc_s, ysc_r, yb_s, yb_r, gram_s, gram_r,
):
    d, e = lax.axis_index("dp"), lax.axis_index("expert")
    tokens, width = grad_ref.shape
    rows = n * cap
    part = scaled_ref.shape[1]
    hid = part * ndp
    tile = min(256, part)
    tiles, per_part = hid // tile, part // tile
    own = n // 2
    members = n // GROUPS
    group_rows = members * cap
    chunk = min(512, width)

    def block(j):
        return pl.ds(pl.multiple_of(j * cap, 16), cap)

    def ahead(j):
        return lax.rem(e + lax.rem(j + n // 2, n), n)

    def behind(j):
        return lax.rem(e + n - lax.rem(j + n // 2, n), n)

    def loop(lo, hi, body):
        def step(i, carry):
            body(i)
            return carry
        lax.fori_loop(lo, hi, step, 0)

    def others(body):
        loop(0, own, body)
        loop(own + 1, n, body)

    def dp_peer(p):
        return lax.rem(d + p, ndp)

    barrier = pltpu.get_barrier_semaphore()

    def greet(j):
        pl.semaphore_signal(barrier, inc=1, device_id=(d, ahead(j)), device_id_type=MESH)

    others(greet)
    for p in range(1, ndp):
        pl.semaphore_signal(barrier, inc=1, device_id=(dp_peer(p), e), device_id_type=MESH)

    expert_row = lax.broadcasted_iota(jnp.int32, (n, tokens), 0)
    is0 = ids_ref[0:1, :] == expert_row
    is1 = ids_ref[1:2, :] == expert_row
    named = (jnp.where(is0, 1.0, 0.0) + jnp.where(is1, 1.0, 0.0)).astype(BF16)
    earlier = lax.broadcasted_iota(jnp.int32, (tokens, tokens), 0) < lax.broadcasted_iota(
        jnp.int32, (tokens, tokens), 1
    )
    rank = dot(named, jnp.where(earlier, 1.0, 0.0).astype(BF16))
    rank0[...] = jnp.where(is0, rank, -1.0)
    rank1[...] = jnp.where(is1, rank, -1.0)

    def build(j):
        to = ahead(j)
        slot = lax.broadcasted_iota(jnp.int32, (cap, tokens), 0).astype(F32)
        for k, ref in ((0, rank0), (1, rank1)):
            select[block(j), k * tokens:(k + 1) * tokens] = jnp.where(
                ref[pl.ds(to, 1), :] == slot, 1.0, 0.0
            ).astype(BF16)

    loop(0, n, build)
    pl.semaphore_wait(barrier, n - 1 + ndp - 1)

    def scaled_copy(j, peer):
        return pltpu.make_async_remote_copy(
            src_ref=send_scaled.at[block(j)], dst_ref=got_scaled.at[d, block(j)],
            send_sem=sc_s.at[j], recv_sem=sc_r.at[j], device_id=(d, peer), device_id_type=MESH)

    def grad_copy(j, peer):
        return pltpu.make_async_remote_copy(
            src_ref=send_grad.at[block(j)], dst_ref=got_grad.at[block(j)],
            send_sem=grad_s.at[j], recv_sem=grad_r.at[j], device_id=(d, peer), device_id_type=MESH)

    def return_copy(j, peer):
        return pltpu.make_async_remote_copy(
            src_ref=summed.at[block(j)], dst_ref=returned.at[block(j)],
            send_sem=ret_s.at[j], recv_sem=ret_r.at[j], device_id=(d, peer), device_id_type=MESH)

    def across_scaled(g, p):
        at = pl.ds(g * group_rows, group_rows)
        return pltpu.make_async_remote_copy(
            src_ref=got_scaled.at[d, at], dst_ref=got_scaled.at[d, at],
            send_sem=ysc_s.at[p, g], recv_sem=ysc_r.at[p, g],
            device_id=(dp_peer(p), e), device_id_type=MESH)

    def arrived_scaled(g, p):
        at = pl.ds(g * group_rows, group_rows)
        source = lax.rem(d + ndp - p, ndp)
        return pltpu.make_async_remote_copy(
            src_ref=got_scaled.at[source, at], dst_ref=got_scaled.at[source, at],
            send_sem=ysc_s.at[p, g], recv_sem=ysc_r.at[p, g],
            device_id=(dp_peer(p), e), device_id_type=MESH)

    def across_back(g, p):
        at = pl.ds(g * group_rows, group_rows)
        return pltpu.make_async_remote_copy(
            src_ref=back_part.at[dp_peer(p), at], dst_ref=back_got.at[p - 1, at],
            send_sem=yb_s.at[p, g], recv_sem=yb_r.at[p, g],
            device_id=(dp_peer(p), e), device_id_type=MESH)

    def across_gram(i, p):
        at = (pl.ds(i * tile, tile), pl.ds(0, (i + 1) * tile))
        return pltpu.make_async_remote_copy(
            src_ref=gram_part.at[at], dst_ref=gram_got.at[(p - 1,) + at],
            send_sem=gram_s.at[p, i], recv_sem=gram_r.at[p, i],
            device_id=(dp_peer(p), e), device_id_type=MESH)

    def scaled_rows(j):
        return dot(select[block(j), :], scaled_ref[...]).astype(BF16)

    def grad_rows(j):
        chosen = select[block(j), 0:tokens] + select[block(j), tokens:2 * tokens]
        return dot(chosen, grad_ref[...]).astype(BF16)

    def put_scaled(j):
        send_scaled[block(j), :] = scaled_rows(j)
        scaled_copy(j, ahead(j)).start()

    def put_grad(j):
        send_grad[block(j), :] = grad_rows(j)
        grad_copy(j, ahead(j)).start()

    others(put_scaled)
    others(put_grad)
    got_scaled[d, own * cap:(own + 1) * cap, :] = scaled_rows(own)
    got_grad[own * cap:(own + 1) * cap, :] = grad_rows(own)

    def members_of(g, body):
        first = g * members
        loop(first + (1 if first == own else 0), first + members, body)

    for g in range(GROUPS):
        members_of(g, lambda j: scaled_copy(j, ahead(j)).wait_recv())
        for p in range(1, ndp):
            across_scaled(g, p).start()

    def back_of(g):
        at = slice(g * group_rows, (g + 1) * group_rows)
        members_of(g, lambda j: grad_copy(j, ahead(j)).wait_recv())

        def column(i):
            term = dot(got_grad[at, :], weight_ref[pl.ds(pl.multiple_of(i * tile, tile), tile), :],
                       ((1,), (1,))).astype(BF16)
            cols = pl.ds(pl.multiple_of(lax.rem(i, per_part) * tile, tile), tile)
            back_part[lax.div(i, per_part), at, cols] = term

        loop(0, tiles, column)
        for p in range(1, ndp):
            across_back(g, p).start()

    for g in range(GROUPS):
        if g == GROUPS - 1:
            for h in range(GROUPS):
                for p in range(1, ndp):
                    arrived_scaled(h, p).wait_recv()
            for b in range(ndp):
                scaled_t[b * part:(b + 1) * part, :] = got_scaled[b].T
        back_of(g)

    for i in range(tiles):
        at = slice(i * tile, (i + 1) * tile)

        def gradient(c):
            cols = pl.ds(pl.multiple_of(c * chunk, chunk), chunk)
            g_ref[at, cols] = dot(scaled_t[at, :], got_grad[:, cols]).astype(BF16)

        def gram(j):
            other = pl.ds(pl.multiple_of(j * tile, tile), tile)
            gram_part[at, other] = dot(g_ref[at, :], g_ref[other, :], ((1,), (1,))).astype(BF16)

        loop(0, width // chunk, gradient)
        loop(0, i + 1, gram)
        for p in range(1, ndp):
            across_gram(i, p).start()

    for g in range(GROUPS):
        at = slice(g * group_rows, (g + 1) * group_rows)
        for p in range(1, ndp):
            across_back(g, p).wait_recv()
        total = back_part[d, at, :].astype(F32)
        for p in range(1, ndp):
            total = total + back_got[p - 1, at, :].astype(F32)
        summed[at, :] = total.astype(BF16)
        members_of(g, lambda j: return_copy(j, behind(j)).start())
    returned[own * cap:(own + 1) * cap, :] = summed[own * cap:(own + 1) * cap, :]

    squares = jnp.zeros((1, 1), F32)
    for i in range(tiles):
        at = slice(i * tile, (i + 1) * tile)
        for p in range(1, ndp):
            across_gram(i, p).wait_recv()
        for j in range(i + 1):
            other = slice(j * tile, (j + 1) * tile)
            total = gram_part[at, other].astype(F32)
            for p in range(1, ndp):
                total = total + gram_got[p - 1, at, other].astype(F32)
            gram_sum[at, other] = total
            here = jnp.sum(jnp.sum(total * total, axis=0, keepdims=True), axis=1, keepdims=True)
            squares = squares + here * (1.0 if i == j else 2.0)
    norm_sq = jnp.sqrt(squares) + 1e-6
    inverse = 1.0 / norm_sq
    scale = lax.rsqrt(norm_sq) * (D**0.5)
    c_ref[...] = jnp.broadcast_to(2.25 * scale, c_ref.shape)
    for i in range(tiles):
        at = slice(i * tile, (i + 1) * tile)
        for j in range(i + 1):
            other = slice(j * tile, (j + 1) * tile)
            value = gram_sum[at, other] * inverse
            a_ref[at, other] = value.astype(BF16)
            if j < i:
                a_ref[other, at] = value.T.astype(BF16)

    def square(i):
        at = pl.ds(pl.multiple_of(i * tile, tile), tile)
        a2 = dot(a_ref[at, :], a_ref[...])
        a1 = a_ref[at, :].astype(F32)
        a2_ref[at, :] = a2.astype(BF16)
        w_ref[at, :] = (1.125 * a1 - 0.125 * a2).astype(BF16)
        gram_sum[at, :] = 1.6875 * a2 - 2.4375 * a1

    def finish(i):
        at = pl.ds(pl.multiple_of(i * tile, tile), tile)
        last = dot(a2_ref[at, :], w_ref[...])
        p_ref[at, :] = ((gram_sum[at, :] - 0.5 * last) * scale).astype(BF16)

    loop(0, tiles, square)
    loop(0, tiles, finish)

    others(lambda j: return_copy(j, behind(j)).wait_recv())
    step = min(256, tokens)

    def pick(t):
        cols = pl.ds(pl.multiple_of(t * step, step), step)
        picked_ref[cols, :] = dot(select[:, cols], returned[...], ((0,), (0,))).astype(BF16)

    loop(0, 2 * tokens // step, pick)

    def drain(j):
        scaled_copy(j, ahead(j)).wait_send()
        grad_copy(j, ahead(j)).wait_send()
        return_copy(j, behind(j)).wait_send()

    others(drain)
    for p in range(1, ndp):
        for g in range(GROUPS):
            across_scaled(g, p).wait_send()
            across_back(g, p).wait_send()
        for i in range(tiles):
            across_gram(i, p).wait_send()


def per_device(n, ndp, grad_out, hidden, gate_prob, expert_ids, weights):
    tokens, width = grad_out.shape
    top = expert_ids.shape[1]
    part = hidden.shape[2]
    hid = part * ndp
    capacity = 5 * tokens * top // (4 * n)
    cap = -(-capacity // 16) * 16
    rows = n * cap
    tiles = hid // min(256, part)
    scaled = (gate_prob[:, :, None] * hidden.astype(F32)).astype(BF16)
    scaled = scaled.transpose(1, 0, 2).reshape(top * tokens, part)
    vmem = pl.BlockSpec(memory_space=pltpu.VMEM)
    dma = pltpu.SemaphoreType.DMA
    grads, poly, scale, picked = pl.pallas_call(
        functools.partial(kernel, n, ndp, cap),
        out_shape=[
            jax.ShapeDtypeStruct((hid, width), BF16),
            jax.ShapeDtypeStruct((hid, hid), BF16),
            jax.ShapeDtypeStruct((8, 128), F32),
            jax.ShapeDtypeStruct((top * tokens, part), BF16),
        ],
        in_specs=[vmem] * 4,
        out_specs=[vmem] * 4,
        scratch_shapes=[
            pltpu.VMEM((n, tokens), F32),
            pltpu.VMEM((n, tokens), F32),
            pltpu.VMEM((rows, top * tokens), BF16),
            pltpu.VMEM((rows, width), BF16),
            pltpu.VMEM((rows, width), BF16),
            pltpu.VMEM((rows, part), BF16),
            pltpu.VMEM((ndp, rows, part), BF16),
            pltpu.VMEM((hid, rows), BF16),
            pltpu.VMEM((ndp, rows, part), BF16),
            pltpu.VMEM((ndp - 1, rows, part), BF16),
            pltpu.VMEM((rows, part), BF16),
            pltpu.VMEM((rows, part), BF16),
            pltpu.VMEM((hid, hid), BF16),
            pltpu.VMEM((ndp - 1, hid, hid), BF16),
            pltpu.VMEM((hid, hid), F32),
            pltpu.VMEM((hid, hid), BF16),
            pltpu.VMEM((hid, hid), BF16),
            pltpu.VMEM((hid, hid), BF16),
        ] + [dma((n,))] * 6 + [dma((ndp, GROUPS))] * 4 + [dma((ndp, tiles))] * 2,
        compiler_params=pltpu.CompilerParams(
            collective_id=0, has_side_effects=True, vmem_limit_bytes=62 * 1024 * 1024
        ),
        cost_estimate=pl.CostEstimate(flops=20_000_000_000, bytes_accessed=16_000_000, transcendentals=0),
    )(expert_ids.T, grad_out, scaled, weights[0])
    update = dot(poly, grads) + grads.astype(F32) * scale[0, 0]
    back = picked.reshape(top, tokens, part).transpose(1, 0, 2).astype(F32)
    hidden_grad = (gate_prob[:, :, None] * back).astype(BF16)
    return (hidden_grad, update[None])


def solution(mesh):
    in_specs = (
        P("expert", "dp"),
        P("expert", None, "dp"),
        P("expert", None),
        P("expert", None),
        P("expert", None, "dp"),
    )
    out_specs = (P("expert", None, "dp"), P("expert", None, "dp"))
    return jax.shard_map(
        functools.partial(per_device, mesh.shape["expert"], mesh.shape["dp"]),
        mesh=mesh, in_specs=in_specs, out_specs=out_specs, check_vma=False,
    )
```

time: 561 us -> 228 us (0.41); the launches traced: 554 us -> 228 us
  waiting for transfers between devices: 225 us -> 0 us
  Pallas kernels: 0 us -> 210 us
  blocking collectives: 197 us -> 0 us
  local copies, waits for them, and re-layouts: 47.6 us -> 3.22 us
  matrix products: 50.4 us -> 7.37 us
  between operations: 14.9 us -> 0.67 us
  other arithmetic: 13.1 us -> 6.52 us
  starting transfers between devices: 6.53 us -> 0 us
    pallas_call x0 -> x1, Pallas kernels: none -> 210 us  [per_device(): pl.pallas_call(functools.partial(kernel, n, ndp, cap), out_shape=[jax.Sha...]
    all_to_all x2 -> x0, blocking collectives: 197 us -> none  [the longest x1 122 us: per_device(): lax.all_to_all(send_grad, 'expert', split_axis=0, concat_axis=0, tiled=True)]
    psum x2 -> x0, waiting for transfers between devices: 125 us -> none  [gram_sum(): return lax.psum(partial_gram.astype(jnp.bfloat16), 'dp').astype(jnp.float32)]
    dot_general x6 -> x1, matrix products: 50.4 us -> 7.37 us  [dot(): return lax.dot_general(a, b, (dims, ((), ())), preferred_element_type=F32)]
    reduce_scatter x1 -> x0, waiting for transfers between devices: 37.7 us -> none  [per_device(): lax.psum_scatter(back_term.astype(jnp.bfloat16), 'dp', scatter_dimension=...]
    all_gather x1 -> x0, waiting for transfers between devices: 31.7 us -> none  [per_device(): whole_scaled = lax.all_gather(scaled_part, 'dp', axis=2, tiled=True)]
    all_to_all x1 -> x0, waiting for transfers between devices: 30.4 us -> none  [per_device(): lax.all_to_all(summed.reshape(experts, capacity, -1).astype(jnp.bfloat16)...]
    scatter x2 -> x0, local copies, waits for them, and re-layouts: 30.2 us -> none  [place_slots(): return empty_rows.at[slot_index].set(values)]
  transfers between devices with their start and end apart: 5 -> 0, of which waited for: 5 -> 0; matrix products, arithmetic and copies ran while one was open for 0% -> 0% of each run, Pallas kernels for 0% -> 0%
where the time goes in v1:
time: 228 us
  Pallas kernels  210 us (92%)
  matrix products  7.37 us (3%)
  other arithmetic  6.52 us (3%)
  local copies, waits for them, and re-layouts  3.22 us (1%)
    pallas_call x1, Pallas kernels, per_device(): pl.pallas_call(functools.partial(kernel, n, ndp, cap), out_shape=[jax.Sha...  210 us
    dot_general x1, matrix products, dot(): return lax.dot_general(a, b, (dims, ((), ())), preferred_element_type=F32)  7.37 us

profile of v1, /device:TPU:11, one launch (start us, length us, event | category | flops | bytes accessed | tf_op | source)
XLA Modules:
  0.0 228.0 jit_solution(4913197201971610473)
XLA Ops:
  0.6 0.8 copy.7
  1.5 2.1 fusion.1
  3.5 1.1 copy.8
  4.7 210.2 %shard_map.68 = (bf16[1024,2048]{1,0:T(8,128)(2,1)}, bf16[1024,1024]{1,0:T(8,128)(2,1)}, f32[8,128]{1,0:T(8,128)}, bf16[1024,512]{1,0:T(8,128)(2,1)}) custom-call(s32[2,512]{1,0:T(2,128)} %bitcast.19, bf16[512,2048]{1,0:T(8,128)(2,1)} %grad_ref.1, bf16[1024,512]{1,0:T(8,128)(2,1)} %bitcast.17, bf16[1024,2048]{1,0:T(8,128)(2,1)} %bitcast.18), custom_call_target="tpu_custom_call" | custom-call | flops 20000000000 | bytes 16000000 | tf_op jit(solution)/shard_map/pallas_call | solution.py:296
  214.9 1.3 slice.3
  216.2 0.0 copy-start
  216.2 1.6 convert.2
  217.8 0.0 copy-start.1
  217.9 2.8 %fusion = bf16[512,2,512]{2,1,0:T(2,128)(2,1)} fusion(f32[2,512,512]{2,1,0:T(8,128)S(1)} %convert.2, f32[512,2]{1,0:T(8,128)S(1)} %copy.7), kind=kLoop, calls=%fused_computation.2 | loop fusion | flops 1048576 | bytes 3149824 | tf_op jit(solution)/shard_map/convert_element_type | solution.py:333
  220.7 0.0 copy-done
  220.7 0.0 copy-done.1
  220.7 7.4 %add_bitcast_fusion = f32[1,1024,2048]{2,1,0:T(8,128)} fusion(bf16[1024,2048]{1,0:T(8,128)(2,1)S(1)} %copy-done, f32[]{:T(128)} %bitcast.6, bf16[1024,1024]{1,0:T(8,128)(2,1)S(1)} %copy-done.1), kind=kOutput, calls=%fused_computation | convolution fusion | flops 4301258752 | bytes 14680068 | tf_op jit(solution)/shard_map/dot_general | solution.py:18
Async XLA Ops:
  216.2 4.5 %copy-start = (bf16[1024,2048]{1,0:T(8,128)(2,1)S(1)}, bf16[1024,2048]{1,0:T(8,128)(2,1)}, u32[]{:S(2)}) copy-start(bf16[1024,2048]{1,0:T(8,128)(2,1)} %get-tuple-element.8) | copy-start | bytes 12582916
  217.8 2.8 %copy-start.1 = (bf16[1024,1024]{1,0:T(8,128)(2,1)S(1)}, bf16[1024,1024]{1,0:T(8,128)(2,1)}, u32[]{:S(2)}) copy-start(bf16[1024,1024]{1,0:T(8,128)(2,1)} %get-tuple-element.7) | copy-start | bytes 6291460

commit v2 on v1

--- a/solution.py
+++ b/solution.py
@@ -20,12 +20,12 @@
 
 def kernel(
     n, ndp, cap,
-    ids_ref, grad_ref, scaled_ref, weight_ref,
+    ids_ref, prob_ref, grad_ref, scaled_ref, weight_ref,
     g_ref, p_ref, c_ref, picked_ref,
-    rank0, rank1, select, send_grad, got_grad, send_scaled, got_scaled, scaled_t,
+    rank0, rank1, select, send_grad, got_grad, send_scaled, got_scaled, early_t, late_t,
     back_part, back_got, summed, returned,
-    gram_part, gram_got, gram_sum, a_ref, a2_ref, w_ref,
-    grad_s, grad_r, sc_s, sc_r, ret_s, ret_r, ysc_s, ysc_r, yb_s, yb_r, gram_s, gram_r,
+    gram_part, gram_got, v_part, v_got, gram_sum, a_ref,
+    grad_s, grad_r, sc_s, sc_r, ret_s, ret_r, ysc_s, ysc_r, yb_s, yb_r, gram_s, gram_r, v_s, v_r,
 ):
     d, e = lax.axis_index("dp"), lax.axis_index("expert")
     tokens, width = grad_ref.shape
@@ -34,19 +34,23 @@
     hid = part * ndp
     tile = min(256, part)
     tiles, per_part = hid // tile, part // tile
-    own = n // 2
+    own = 0
     members = n // GROUPS
     group_rows = members * cap
     chunk = min(512, width)
+    split = rows - group_rows
 
     def block(j):
         return pl.ds(pl.multiple_of(j * cap, 16), cap)
 
+    def offset(j):
+        return lax.rem(j, members) * GROUPS + lax.div(j, members)
+
     def ahead(j):
-        return lax.rem(e + lax.rem(j + n // 2, n), n)
+        return lax.rem(e + offset(j), n)
 
     def behind(j):
-        return lax.rem(e + n - lax.rem(j + n // 2, n), n)
+        return lax.rem(e + n - offset(j), n)
 
     def loop(lo, hi, body):
         def step(i, carry):
@@ -55,8 +59,7 @@
         lax.fori_loop(lo, hi, step, 0)
 
     def others(body):
-        loop(0, own, body)
-        loop(own + 1, n, body)
+        loop(1, n, body)
 
     def dp_peer(p):
         return lax.rem(d + p, ndp)
@@ -136,6 +139,12 @@
             send_sem=gram_s.at[p, i], recv_sem=gram_r.at[p, i],
             device_id=(dp_peer(p), e), device_id_type=MESH)
 
+    def across_v(p):
+        return pltpu.make_async_remote_copy(
+            src_ref=v_part, dst_ref=v_got.at[p - 1],
+            send_sem=v_s.at[p], recv_sem=v_r.at[p],
+            device_id=(dp_peer(p), e), device_id_type=MESH)
+
     def scaled_rows(j):
         return dot(select[block(j), :], scaled_ref[...]).astype(BF16)
 
@@ -151,23 +160,22 @@
         send_grad[block(j), :] = grad_rows(j)
         grad_copy(j, ahead(j)).start()
 
-    others(put_scaled)
-    others(put_grad)
-    got_scaled[d, own * cap:(own + 1) * cap, :] = scaled_rows(own)
-    got_grad[own * cap:(own + 1) * cap, :] = grad_rows(own)
-
     def members_of(g, body):
         first = g * members
         loop(first + (1 if first == own else 0), first + members, body)
 
+    others(put_scaled)
+    members_of(0, put_grad)
+    got_scaled[d, 0:cap, :] = scaled_rows(own)
+    got_grad[0:cap, :] = grad_rows(own)
+    others(lambda j: scaled_copy(j, ahead(j)).wait_recv())
+    members_of(1, put_grad)
     for g in range(GROUPS):
-        members_of(g, lambda j: scaled_copy(j, ahead(j)).wait_recv())
         for p in range(1, ndp):
             across_scaled(g, p).start()
 
     def back_of(g):
         at = slice(g * group_rows, (g + 1) * group_rows)
-        members_of(g, lambda j: grad_copy(j, ahead(j)).wait_recv())
 
         def column(i):
             term = dot(got_grad[at, :], weight_ref[pl.ds(pl.multiple_of(i * tile, tile), tile), :],
@@ -179,21 +187,26 @@
         for p in range(1, ndp):
             across_back(g, p).start()
 
-    for g in range(GROUPS):
-        if g == GROUPS - 1:
+    for g in range(GROUPS - 1):
+        members_of(g, lambda j: grad_copy(j, ahead(j)).wait_recv())
+        if g + 2 < GROUPS:
+            members_of(g + 2, put_grad)
+        if g < GROUPS - 2:
+            back_of(g)
+        if g == GROUPS - 3:
             for h in range(GROUPS):
                 for p in range(1, ndp):
                     arrived_scaled(h, p).wait_recv()
             for b in range(ndp):
-                scaled_t[b * part:(b + 1) * part, :] = got_scaled[b].T
-        back_of(g)
+                early_t[b * part:(b + 1) * part, :] = got_scaled[b, 0:split, :].T
+                late_t[b * part:(b + 1) * part, :] = got_scaled[b, split:rows, :].T
 
     for i in range(tiles):
         at = slice(i * tile, (i + 1) * tile)
 
         def gradient(c):
             cols = pl.ds(pl.multiple_of(c * chunk, chunk), chunk)
-            g_ref[at, cols] = dot(scaled_t[at, :], got_grad[:, cols]).astype(BF16)
+            g_ref[at, cols] = dot(early_t[at, :], got_grad[0:split, cols]).astype(BF16)
 
         def gram(j):
             other = pl.ds(pl.multiple_of(j * tile, tile), tile)
@@ -203,8 +216,9 @@
         loop(0, i + 1, gram)
         for p in range(1, ndp):
             across_gram(i, p).start()
-
-    for g in range(GROUPS):
+    back_of(GROUPS - 2)
+
+    def give_back(g):
         at = slice(g * group_rows, (g + 1) * group_rows)
         for p in range(1, ndp):
             across_back(g, p).wait_recv()
@@ -213,6 +227,50 @@
             total = total + back_got[p - 1, at, :].astype(F32)
         summed[at, :] = total.astype(BF16)
         members_of(g, lambda j: return_copy(j, behind(j)).start())
+
+    members_of(GROUPS - 1, lambda j: grad_copy(j, ahead(j)).wait_recv())
+
+    def halfway(i):
+        at = pl.ds(pl.multiple_of(i * tile, tile), tile)
+
+        def piece(c):
+            cols = pl.ds(pl.multiple_of(c * chunk, chunk), chunk)
+            late = dot(late_t[at, :], got_grad[split:rows, cols])
+            g_ref[at, cols] = (g_ref[at, cols].astype(F32) + 0.5 * late).astype(BF16)
+
+        loop(0, width // chunk, piece)
+        v_part[:, at] = dot(got_grad[split:rows, :], g_ref[at, :], ((1,), (1,))).astype(BF16)
+
+    loop(0, tiles, halfway)
+    for p in range(1, ndp):
+        across_v(p).start()
+    for g in range(GROUPS - 2):
+        give_back(g)
+    back_of(GROUPS - 1)
+    give_back(GROUPS - 2)
+
+    def whole(i):
+        at = pl.ds(pl.multiple_of(i * tile, tile), tile)
+
+        def piece(c):
+            cols = pl.ds(pl.multiple_of(c * chunk, chunk), chunk)
+            g_ref[at, cols] = (
+                dot(early_t[at, :], got_grad[0:split, cols]) + dot(late_t[at, :], got_grad[split:rows, cols])
+            ).astype(BF16)
+
+        loop(0, width // chunk, piece)
+
+    loop(0, tiles, whole)
+    for p in range(1, ndp):
+        across_v(p).wait_recv()
+    v = v_part[...].astype(F32)
+    for p in range(1, ndp):
+        v = v + v_got[p - 1].astype(F32)
+    v_sum = v.astype(BF16)
+    for i in range(tiles):
+        at = slice(i * tile, (i + 1) * tile)
+        gram_sum[at, :] = dot(late_t[at, :], v_sum)
+    give_back(GROUPS - 1)
     returned[own * cap:(own + 1) * cap, :] = summed[own * cap:(own + 1) * cap, :]
 
     squares = jnp.zeros((1, 1), F32)
@@ -225,6 +283,7 @@
             total = gram_part[at, other].astype(F32)
             for p in range(1, ndp):
                 total = total + gram_got[p - 1, at, other].astype(F32)
+            total = total + gram_sum[at, other] + gram_sum[other, at].T
             gram_sum[at, other] = total
             here = jnp.sum(jnp.sum(total * total, axis=0, keepdims=True), axis=1, keepdims=True)
             squares = squares + here * (1.0 if i == j else 2.0)
@@ -241,6 +300,11 @@
             if j < i:
                 a_ref[other, at] = value.T.astype(BF16)
 
+    for p in range(1, ndp):
+        for i in range(tiles):
+            across_gram(i, p).wait_send()
+    a2_ref, w_ref = gram_part, gram_got.at[0]
+
     def square(i):
         at = pl.ds(pl.multiple_of(i * tile, tile), tile)
         a2 = dot(a_ref[at, :], a_ref[...])
@@ -259,12 +323,11 @@
 
     others(lambda j: return_copy(j, behind(j)).wait_recv())
     step = min(256, tokens)
-
-    def pick(t):
-        cols = pl.ds(pl.multiple_of(t * step, step), step)
-        picked_ref[cols, :] = dot(select[:, cols], returned[...], ((0,), (0,))).astype(BF16)
-
-    loop(0, 2 * tokens // step, pick)
+    for k in range(2):
+        for t in range(0, tokens, step):
+            cols = slice(k * tokens + t, k * tokens + t + step)
+            value = dot(select[:, cols], returned[...], ((0,), (0,)))
+            picked_ref[k, t:t + step, :] = (prob_ref[t:t + step, k:k + 1] * value).astype(BF16)
 
     def drain(j):
         scaled_copy(j, ahead(j)).wait_send()
@@ -276,8 +339,7 @@
         for g in range(GROUPS):
             across_scaled(g, p).wait_send()
             across_back(g, p).wait_send()
-        for i in range(tiles):
-            across_gram(i, p).wait_send()
+        across_v(p).wait_send()
 
 
 def per_device(n, ndp, grad_out, hidden, gate_prob, expert_ids, weights):
@@ -288,6 +350,7 @@
     capacity = 5 * tokens * top // (4 * n)
     cap = -(-capacity // 16) * 16
     rows = n * cap
+    late = rows // GROUPS
     tiles = hid // min(256, part)
     scaled = (gate_prob[:, :, None] * hidden.astype(F32)).astype(BF16)
     scaled = scaled.transpose(1, 0, 2).reshape(top * tokens, part)
@@ -299,9 +362,9 @@
             jax.ShapeDtypeStruct((hid, width), BF16),
             jax.ShapeDtypeStruct((hid, hid), BF16),
             jax.ShapeDtypeStruct((8, 128), F32),
-            jax.ShapeDtypeStruct((top * tokens, part), BF16),
+            jax.ShapeDtypeStruct((top, tokens, part), BF16),
         ],
-        in_specs=[vmem] * 4,
+        in_specs=[vmem] * 5,
         out_specs=[vmem] * 4,
         scratch_shapes=[
             pltpu.VMEM((n, tokens), F32),
@@ -311,26 +374,26 @@
             pltpu.VMEM((rows, width), BF16),
             pltpu.VMEM((rows, part), BF16),
             pltpu.VMEM((ndp, rows, part), BF16),
-            pltpu.VMEM((hid, rows), BF16),
+            pltpu.VMEM((hid, rows - late), BF16),
+            pltpu.VMEM((hid, late), BF16),
             pltpu.VMEM((ndp, rows, part), BF16),
             pltpu.VMEM((ndp - 1, rows, part), BF16),
             pltpu.VMEM((rows, part), BF16),
             pltpu.VMEM((rows, part), BF16),
             pltpu.VMEM((hid, hid), BF16),
             pltpu.VMEM((ndp - 1, hid, hid), BF16),
+            pltpu.VMEM((late, hid), BF16),
+            pltpu.VMEM((ndp - 1, late, hid), BF16),
             pltpu.VMEM((hid, hid), F32),
             pltpu.VMEM((hid, hid), BF16),
-            pltpu.VMEM((hid, hid), BF16),
-            pltpu.VMEM((hid, hid), BF16),
-        ] + [dma((n,))] * 6 + [dma((ndp, GROUPS))] * 4 + [dma((ndp, tiles))] * 2,
+        ] + [dma((n,))] * 6 + [dma((ndp, GROUPS))] * 4 + [dma((ndp, tiles))] * 2 + [dma((ndp,))] * 2,
         compiler_params=pltpu.CompilerParams(
             collective_id=0, has_side_effects=True, vmem_limit_bytes=62 * 1024 * 1024
         ),
         cost_estimate=pl.CostEstimate(flops=20_000_000_000, bytes_accessed=16_000_000, transcendentals=0),
-    )(expert_ids.T, grad_out, scaled, weights[0])
+    )(expert_ids.T, gate_prob, grad_out, scaled, weights[0])
     update = dot(poly, grads) + grads.astype(F32) * scale[0, 0]
-    back = picked.reshape(top, tokens, part).transpose(1, 0, 2).astype(F32)
-    hidden_grad = (gate_prob[:, :, None] * back).astype(BF16)
+    hidden_grad = picked.transpose(1, 0, 2)
     return (hidden_grad, update[None])
 
 

time: 228 us -> 234 us (1.026)
  matrix products: 7.37 us -> 12.6 us
  other arithmetic: 6.52 us -> 2.16 us
  local copies, waits for them, and re-layouts: 3.22 us -> 6.5 us
    dot_general x1, matrix products: 7.37 us -> 12.6 us  [dot(): return lax.dot_general(a, b, (dims, ((), ())), preferred_element_type=F32)]
    convert_element_type x2 -> x0, other arithmetic: 4.46 us -> none  [the longest x1 2.81 us: per_device(): hidden_grad = (gate_prob[:, :, None] * back).astype(BF16)]
    unnamed x5 -> x4, local copies, waits for them, and re-layouts: 0.83 us -> 4.1 us
where the time goes in v2:
time: 234 us; the launch traced here: 233 us
  Pallas kernels  211 us (90%)
  matrix products  12.6 us (5%)
  local copies, waits for them, and re-layouts  6.5 us (3%)
    pallas_call x1, Pallas kernels, per_device(): pl.pallas_call(functools.partial(kernel, n, ndp, cap), out_shape=[jax.Sha...  211 us
    dot_general x1, matrix products, dot(): return lax.dot_general(a, b, (dims, ((), ())), preferred_element_type=F32)  12.6 us

profile of v2, /device:TPU:11, one launch (start us, length us, event | category | flops | bytes accessed | tf_op | source)
XLA Modules:
  0.0 232.6 jit_solution(17235167735996855070)
XLA Ops:
  0.6 0.8 copy.9.prob_ref
  1.5 0.0 copy-start
  1.5 2.2 fusion
  3.6 1.1 copy.8
  4.8 0.0 copy-done
  4.8 210.6 %shard_map.68 = (bf16[1024,2048]{1,0:T(8,128)(2,1)}, bf16[1024,1024]{1,0:T(8,128)(2,1)}, f32[8,128]{1,0:T(8,128)}, bf16[2,512,512]{2,1,0:T(8,128)(2,1)}) custom-call(s32[2,512]{1,0:T(2,128)} %bitcast.14, f32[512,2]{1,0:T(8,128)} %copy-done, bf16[512,2048]{1,0:T(8,128)(2,1)} %grad_ref.1, bf16[1024,512]{1,0:T(8,128)(2,1)} %bitcast.12, bf16[1024,2048]{1,0:T(8,128)(2,1)} %bitcast.13), custom_call_target="tpu_custom_call" | custom-call | flops 20000000000 | bytes 16000000 | tf_op jit(solution)/shard_map/pallas_call | solution.py:359
  215.4 1.3 slice.3
  216.6 3.3 %copy.10 = bf16[512,2,512]{2,1,0:T(2,128)(2,1)} copy(bf16[512,2,512]{2,0,1:T(8,128)(2,1)} %bitcast.11) | data formatting | bytes 2097152
  219.9 12.6 %add_bitcast_fusion = f32[1,1024,2048]{2,1,0:T(8,128)} fusion(bf16[1024,2048]{1,0:T(8,128)(2,1)} %get-tuple-element.8, f32[]{:T(128)} %bitcast.5, bf16[1024,1024]{1,0:T(8,128)(2,1)} %get-tuple-element.7), kind=kOutput, calls=%fused_computation | convolution fusion | flops 4301258752 | bytes 14680068 | tf_op jit(solution)/shard_map/dot_general | solution.py:18
Async XLA Ops:
  1.5 3.3 %copy-start = (f32[512,2]{1,0:T(8,128)}, f32[512,2]{1,0:T(8,128)S(1)}, u32[]{:S(2)}) copy-start(f32[512,2]{1,0:T(8,128)S(1)} %copy.9.prob_ref) | copy-start | bytes 12292

commit v3 on v2

--- a/solution.py
+++ b/solution.py
@@ -165,11 +165,10 @@
         loop(first + (1 if first == own else 0), first + members, body)
 
     others(put_scaled)
-    members_of(0, put_grad)
+    others(put_grad)
     got_scaled[d, 0:cap, :] = scaled_rows(own)
     got_grad[0:cap, :] = grad_rows(own)
     others(lambda j: scaled_copy(j, ahead(j)).wait_recv())
-    members_of(1, put_grad)
     for g in range(GROUPS):
         for p in range(1, ndp):
             across_scaled(g, p).start()
@@ -189,8 +188,6 @@
 
     for g in range(GROUPS - 1):
         members_of(g, lambda j: grad_copy(j, ahead(j)).wait_recv())
-        if g + 2 < GROUPS:
-            members_of(g + 2, put_grad)
         if g < GROUPS - 2:
             back_of(g)
         if g == GROUPS - 3:
@@ -340,6 +337,11 @@
             across_scaled(g, p).wait_send()
             across_back(g, p).wait_send()
         across_v(p).wait_send()
+
+
+def update_kernel(c_ref, p_ref, g_ref, out_ref):
+    grads = g_ref[...]
+    out_ref[...] = dot(p_ref[...], grads) + grads.astype(F32) * c_ref[0:1, 0:1]
 
 
 def per_device(n, ndp, grad_out, hidden, gate_prob, expert_ids, weights):
@@ -392,7 +394,21 @@
         ),
         cost_estimate=pl.CostEstimate(flops=20_000_000_000, bytes_accessed=16_000_000, transcendentals=0),
     )(expert_ids.T, gate_prob, grad_out, scaled, weights[0])
-    update = dot(poly, grads) + grads.astype(F32) * scale[0, 0]
+    chunk = min(256, width)
+    update = pl.pallas_call(
+        update_kernel,
+        grid=(width // chunk,),
+        out_shape=jax.ShapeDtypeStruct((hid, width), F32),
+        in_specs=[
+            pl.BlockSpec((8, 128), lambda c: (0, 0)),
+            pl.BlockSpec((hid, hid), lambda c: (0, 0)),
+            pl.BlockSpec((hid, chunk), lambda c: (0, c)),
+        ],
+        out_specs=pl.BlockSpec((hid, chunk), lambda c: (0, c)),
+        compiler_params=pltpu.CompilerParams(vmem_limit_bytes=24 * 1024 * 1024),
+        cost_estimate=pl.CostEstimate(
+            flops=2 * hid * hid * width, bytes_accessed=6 * hid * width, transcendentals=0),
+    )(scale, poly, grads)
     hidden_grad = picked.transpose(1, 0, 2)
     return (hidden_grad, update[None])
 

time: 234 us -> 229 us (0.979)
  matrix products: 12.6 us -> 0 us
  Pallas kernels: 211 us -> 218 us
    dot_general x1 -> x0, matrix products: 12.6 us -> none  [dot(): return lax.dot_general(a, b, (dims, ((), ())), preferred_element_type=F32)]
    pallas_call x0 -> x1, Pallas kernels: none -> 7.86 us  [per_device(): pl.pallas_call(update_kernel, grid=(width // chunk,), out_shape=jax.Shape...]
    unnamed x4 -> x10, local copies, waits for them, and re-layouts: 4.1 us -> 6.45 us
where the time goes in v3:
time: 229 us
  Pallas kernels  218 us (95%)
  local copies, waits for them, and re-layouts  7.58 us (3%)
    pallas_call x1, Pallas kernels, per_device(): pl.pallas_call(functools.partial(kernel, n, ndp, cap), out_shape=[jax.Sha...  211 us
    pallas_call x1, Pallas kernels, per_device(): pl.pallas_call(update_kernel, grid=(width // chunk,), out_shape=jax.Shape...  7.86 us
    unnamed x10, local copies, waits for them, and re-layouts  6.45 us

profile of v3, /device:TPU:11, one launch (start us, length us, event | category | flops | bytes accessed | tf_op | source)
XLA Modules:
  0.0 228.9 jit_solution(1454052218431112762)
XLA Ops:
  0.6 0.8 copy.9.prob_ref
  1.5 0.0 copy-start.3
  1.5 2.2 fusion
  3.6 1.1 copy.8
  4.8 0.0 copy-done.3
  4.8 210.6 %shard_map.68 = (bf16[1024,2048]{1,0:T(8,128)(2,1)}, bf16[1024,1024]{1,0:T(8,128)(2,1)}, f32[8,128]{1,0:T(8,128)}, bf16[2,512,512]{2,1,0:T(8,128)(2,1)}) custom-call(s32[2,512]{1,0:T(2,128)} %bitcast.10, f32[512,2]{1,0:T(8,128)} %copy-done.3, bf16[512,2048]{1,0:T(8,128)(2,1)} %grad_ref.1, bf16[1024,512]{1,0:T(8,128)(2,1)} %bitcast.7, bf16[1024,2048]{1,0:T(8,128)(2,1)} %bitcast.9), custom_call_target="tpu_custom_call" | custom-call | flops 20000000000 | bytes 16000000 | tf_op jit(solution)/shard_map/pallas_call | solution.py:361
  215.4 0.0 copy-start.1
  215.4 0.0 copy-start.2
  215.4 3.4 %copy.10 = bf16[512,2,512]{2,1,0:T(2,128)(2,1)} copy(bf16[512,2,512]{2,0,1:T(8,128)(2,1)} %bitcast.8) | data formatting | bytes 2097152
  218.8 0.0 copy-done.1
  218.8 0.0 copy-done.2
  218.8 0.0 copy-start
  218.8 2.2 copy-done
  221.0 7.9 %shard_map.69 = f32[1024,2048]{1,0:T(8,128)} custom-call(f32[8,128]{1,0:T(8,128)S(1)} %copy-done.2, bf16[1024,1024]{1,0:T(8,128)(2,1)S(1)} %copy-done.1, bf16[1024,2048]{1,0:T(8,128)(2,1)S(1)} %copy-done), custom_call_target="tpu_custom_call" | custom-call | flops 4294967296 | bytes 12582912 | tf_op jit(solution)/shard_map/pallas_call | solution.py:398
Async XLA Ops:
  1.5 3.3 %copy-start.3 = (f32[512,2]{1,0:T(8,128)}, f32[512,2]{1,0:T(8,128)S(1)}, u32[]{:S(2)}) copy-start(f32[512,2]{1,0:T(8,128)S(1)} %copy.9.prob_ref) | copy-start | bytes 12292
  215.4 3.4 %copy-start.1 = (bf16[1024,1024]{1,0:T(8,128)(2,1)S(1)}, bf16[1024,1024]{1,0:T(8,128)(2,1)}, u32[]{:S(2)}) copy-start(bf16[1024,1024]{1,0:T(8,128)(2,1)} %get-tuple-element.8.p_ref) | copy-start | bytes 6291460
  215.4 3.4 %copy-start.2 = (f32[8,128]{1,0:T(8,128)S(1)}, f32[8,128]{1,0:T(8,128)}, u32[]{:S(2)}) copy-start(f32[8,128]{1,0:T(8,128)} %get-tuple-element.7.c_ref) | copy-start | bytes 12292
  218.8 2.2 copy-start

commit v4 on v3

--- a/solution.py
+++ b/solution.py
@@ -165,7 +165,16 @@
         loop(first + (1 if first == own else 0), first + members, body)
 
     others(put_scaled)
-    others(put_grad)
+    window = members * 3 // 2
+    first_stop = window + members
+    stops = (first_stop, first_stop + members, n)
+
+    def put_later(j):
+        send_grad[block(j), :] = grad_rows(j)
+        grad_copy(j - window, ahead(j - window)).wait_send()
+        grad_copy(j, ahead(j)).start()
+
+    loop(1, window + 1, put_grad)
     got_scaled[d, 0:cap, :] = scaled_rows(own)
     got_grad[0:cap, :] = grad_rows(own)
     others(lambda j: scaled_copy(j, ahead(j)).wait_recv())
@@ -187,6 +196,7 @@
             across_back(g, p).start()
 
     for g in range(GROUPS - 1):
+        loop(window + 1 if g == 0 else stops[g - 1], stops[g], put_later)
         members_of(g, lambda j: grad_copy(j, ahead(j)).wait_recv())
         if g < GROUPS - 2:
             back_of(g)
@@ -227,6 +237,8 @@
 
     members_of(GROUPS - 1, lambda j: grad_copy(j, ahead(j)).wait_recv())
 
+    back_of(GROUPS - 1)
+
     def halfway(i):
         at = pl.ds(pl.multiple_of(i * tile, tile), tile)
 
@@ -241,10 +253,8 @@
     loop(0, tiles, halfway)
     for p in range(1, ndp):
         across_v(p).start()
-    for g in range(GROUPS - 2):
+    for g in range(GROUPS - 1):
         give_back(g)
-    back_of(GROUPS - 1)
-    give_back(GROUPS - 2)
 
     def whole(i):
         at = pl.ds(pl.multiple_of(i * tile, tile), tile)
@@ -258,6 +268,7 @@
         loop(0, width // chunk, piece)
 
     loop(0, tiles, whole)
+    give_back(GROUPS - 1)
     for p in range(1, ndp):
         across_v(p).wait_recv()
     v = v_part[...].astype(F32)
@@ -267,7 +278,6 @@
     for i in range(tiles):
         at = slice(i * tile, (i + 1) * tile)
         gram_sum[at, :] = dot(late_t[at, :], v_sum)
-    give_back(GROUPS - 1)
     returned[own * cap:(own + 1) * cap, :] = summed[own * cap:(own + 1) * cap, :]
 
     squares = jnp.zeros((1, 1), F32)
@@ -328,10 +338,10 @@
 
     def drain(j):
         scaled_copy(j, ahead(j)).wait_send()
-        grad_copy(j, ahead(j)).wait_send()
         return_copy(j, behind(j)).wait_send()
 
     others(drain)
+    loop(n - window, n, lambda j: grad_copy(j, ahead(j)).wait_send())
     for p in range(1, ndp):
         for g in range(GROUPS):
             across_scaled(g, p).wait_send()

time: 229 us -> 231 us (level)
  no operation moved by 1% of the time
where the time goes in v4:
time: 231 us; the launch traced here: 230 us
  Pallas kernels  220 us (95%)
  local copies, waits for them, and re-layouts  7.58 us (3%)
    pallas_call x1, Pallas kernels, per_device(): pl.pallas_call(functools.partial(kernel, n, ndp, cap), out_shape=[jax.Sha...  212 us
    pallas_call x1, Pallas kernels, per_device(): pl.pallas_call(update_kernel, grid=(width // chunk,), out_shape=jax.Shape...  7.86 us
    unnamed x10, local copies, waits for them, and re-layouts  6.45 us

profile of v4, /device:TPU:11, one launch (start us, length us, event | category | flops | bytes accessed | tf_op | source)
XLA Modules:
  0.0 230.1 jit_solution(1165722216077315096)
XLA Ops:
  0.6 0.8 copy.9.prob_ref
  1.5 0.0 copy-start.3
  1.5 2.2 fusion
  3.6 1.1 copy.8
  4.8 0.0 copy-done.3
  4.8 211.8 %shard_map.68 = (bf16[1024,2048]{1,0:T(8,128)(2,1)}, bf16[1024,1024]{1,0:T(8,128)(2,1)}, f32[8,128]{1,0:T(8,128)}, bf16[2,512,512]{2,1,0:T(8,128)(2,1)}) custom-call(s32[2,512]{1,0:T(2,128)} %bitcast.10, f32[512,2]{1,0:T(8,128)} %copy-done.3, bf16[512,2048]{1,0:T(8,128)(2,1)} %grad_ref.1, bf16[1024,512]{1,0:T(8,128)(2,1)} %bitcast.7, bf16[1024,2048]{1,0:T(8,128)(2,1)} %bitcast.9), custom_call_target="tpu_custom_call" | custom-call | flops 20000000000 | bytes 16000000 | tf_op jit(solution)/shard_map/pallas_call | solution.py:371
  216.6 0.0 copy-start.1
  216.6 0.0 copy-start.2
  216.6 3.4 %copy.10 = bf16[512,2,512]{2,1,0:T(2,128)(2,1)} copy(bf16[512,2,512]{2,0,1:T(8,128)(2,1)} %bitcast.8) | data formatting | bytes 2097152
  220.0 0.0 copy-done.1
  220.0 0.0 copy-done.2
  220.0 0.0 copy-start
  220.0 2.2 copy-done
  222.2 7.9 %shard_map.69 = f32[1024,2048]{1,0:T(8,128)} custom-call(f32[8,128]{1,0:T(8,128)S(1)} %copy-done.2, bf16[1024,1024]{1,0:T(8,128)(2,1)S(1)} %copy-done.1, bf16[1024,2048]{1,0:T(8,128)(2,1)S(1)} %copy-done), custom_call_target="tpu_custom_call" | custom-call | flops 4294967296 | bytes 12582912 | tf_op jit(solution)/shard_map/pallas_call | solution.py:408
Async XLA Ops:
  1.5 3.3 %copy-start.3 = (f32[512,2]{1,0:T(8,128)}, f32[512,2]{1,0:T(8,128)S(1)}, u32[]{:S(2)}) copy-start(f32[512,2]{1,0:T(8,128)S(1)} %copy.9.prob_ref) | copy-start | bytes 12292
  216.6 3.4 %copy-start.1 = (bf16[1024,1024]{1,0:T(8,128)(2,1)S(1)}, bf16[1024,1024]{1,0:T(8,128)(2,1)}, u32[]{:S(2)}) copy-start(bf16[1024,1024]{1,0:T(8,128)(2,1)} %get-tuple-element.8.p_ref) | copy-start | bytes 6291460
  216.6 3.4 %copy-start.2 = (f32[8,128]{1,0:T(8,128)S(1)}, f32[8,128]{1,0:T(8,128)}, u32[]{:S(2)}) copy-start(f32[8,128]{1,0:T(8,128)} %get-tuple-element.7.c_ref) | copy-start | bytes 12292
  220.0 2.2 copy-start

commit v5 on v4

--- a/solution.py
+++ b/solution.py
@@ -22,10 +22,10 @@
     n, ndp, cap,
     ids_ref, prob_ref, grad_ref, scaled_ref, weight_ref,
     g_ref, p_ref, c_ref, picked_ref,
-    rank0, rank1, select, send_grad, got_grad, send_scaled, got_scaled, early_t, late_t,
+    rank0, rank1, select, send_grad, got_grad, send_scaled, got_scaled, scaled_t,
     back_part, back_got, summed, returned,
-    gram_part, gram_got, v_part, v_got, gram_sum, a_ref,
-    grad_s, grad_r, sc_s, sc_r, ret_s, ret_r, ysc_s, ysc_r, yb_s, yb_r, gram_s, gram_r, v_s, v_r,
+    gram_part, gram_got, gram_sum, a_ref,
+    grad_s, grad_r, sc_s, sc_r, ret_s, ret_r, ysc_s, ysc_r, yb_s, yb_r, gram_s, gram_r,
 ):
     d, e = lax.axis_index("dp"), lax.axis_index("expert")
     tokens, width = grad_ref.shape
@@ -38,13 +38,12 @@
     members = n // GROUPS
     group_rows = members * cap
     chunk = min(512, width)
-    split = rows - group_rows
 
     def block(j):
         return pl.ds(pl.multiple_of(j * cap, 16), cap)
 
     def offset(j):
-        return lax.rem(j, members) * GROUPS + lax.div(j, members)
+        return (lax.rem(j + n // 2 - 2, n - 1) + 1) * lax.div(j + n - 1, n)
 
     def ahead(j):
         return lax.rem(e + offset(j), n)
@@ -139,12 +138,6 @@
             send_sem=gram_s.at[p, i], recv_sem=gram_r.at[p, i],
             device_id=(dp_peer(p), e), device_id_type=MESH)
 
-    def across_v(p):
-        return pltpu.make_async_remote_copy(
-            src_ref=v_part, dst_ref=v_got.at[p - 1],
-            send_sem=v_s.at[p], recv_sem=v_r.at[p],
-            device_id=(dp_peer(p), e), device_id_type=MESH)
-
     def scaled_rows(j):
         return dot(select[block(j), :], scaled_ref[...]).astype(BF16)
 
@@ -198,22 +191,36 @@
     for g in range(GROUPS - 1):
         loop(window + 1 if g == 0 else stops[g - 1], stops[g], put_later)
         members_of(g, lambda j: grad_copy(j, ahead(j)).wait_recv())
-        if g < GROUPS - 2:
-            back_of(g)
+        back_of(g)
         if g == GROUPS - 3:
             for h in range(GROUPS):
                 for p in range(1, ndp):
                     arrived_scaled(h, p).wait_recv()
             for b in range(ndp):
-                early_t[b * part:(b + 1) * part, :] = got_scaled[b, 0:split, :].T
-                late_t[b * part:(b + 1) * part, :] = got_scaled[b, split:rows, :].T
+                scaled_t[b * part:(b + 1) * part, :] = got_scaled[b].T
+
+    def give_back(g):
+        at = slice(g * group_rows, (g + 1) * group_rows)
+        for p in range(1, ndp):
+            across_back(g, p).wait_recv()
+        total = back_part[d, at, :].astype(F32)
+        for p in range(1, ndp):
+            total = total + back_got[p - 1, at, :].astype(F32)
+        summed[at, :] = total.astype(BF16)
+        members_of(g, lambda j: return_copy(j, behind(j)).start())
+
+    members_of(GROUPS - 1, lambda j: grad_copy(j, ahead(j)).wait_recv())
+
+    for g in range(GROUPS - 1):
+        give_back(g)
+    back_of(GROUPS - 1)
 
     for i in range(tiles):
         at = slice(i * tile, (i + 1) * tile)
 
         def gradient(c):
             cols = pl.ds(pl.multiple_of(c * chunk, chunk), chunk)
-            g_ref[at, cols] = dot(early_t[at, :], got_grad[0:split, cols]).astype(BF16)
+            g_ref[at, cols] = dot(scaled_t[at, :], got_grad[:, cols]).astype(BF16)
 
         def gram(j):
             other = pl.ds(pl.multiple_of(j * tile, tile), tile)
@@ -223,61 +230,7 @@
         loop(0, i + 1, gram)
         for p in range(1, ndp):
             across_gram(i, p).start()
-    back_of(GROUPS - 2)
-
-    def give_back(g):
-        at = slice(g * group_rows, (g + 1) * group_rows)
-        for p in range(1, ndp):
-            across_back(g, p).wait_recv()
-        total = back_part[d, at, :].astype(F32)
-        for p in range(1, ndp):
-            total = total + back_got[p - 1, at, :].astype(F32)
-        summed[at, :] = total.astype(BF16)
-        members_of(g, lambda j: return_copy(j, behind(j)).start())
-
-    members_of(GROUPS - 1, lambda j: grad_copy(j, ahead(j)).wait_recv())
-
-    back_of(GROUPS - 1)
-
-    def halfway(i):
-        at = pl.ds(pl.multiple_of(i * tile, tile), tile)
-
-        def piece(c):
-            cols = pl.ds(pl.multiple_of(c * chunk, chunk), chunk)
-            late = dot(late_t[at, :], got_grad[split:rows, cols])
-            g_ref[at, cols] = (g_ref[at, cols].astype(F32) + 0.5 * late).astype(BF16)
-
-        loop(0, width // chunk, piece)
-        v_part[:, at] = dot(got_grad[split:rows, :], g_ref[at, :], ((1,), (1,))).astype(BF16)
-
-    loop(0, tiles, halfway)
-    for p in range(1, ndp):
-        across_v(p).start()
-    for g in range(GROUPS - 1):
-        give_back(g)
-
-    def whole(i):
-        at = pl.ds(pl.multiple_of(i * tile, tile), tile)
-
-        def piece(c):
-            cols = pl.ds(pl.multiple_of(c * chunk, chunk), chunk)
-            g_ref[at, cols] = (
-                dot(early_t[at, :], got_grad[0:split, cols]) + dot(late_t[at, :], got_grad[split:rows, cols])
-            ).astype(BF16)
-
-        loop(0, width // chunk, piece)
-
-    loop(0, tiles, whole)
     give_back(GROUPS - 1)
-    for p in range(1, ndp):
-        across_v(p).wait_recv()
-    v = v_part[...].astype(F32)
-    for p in range(1, ndp):
-        v = v + v_got[p - 1].astype(F32)
-    v_sum = v.astype(BF16)
-    for i in range(tiles):
-        at = slice(i * tile, (i + 1) * tile)
-        gram_sum[at, :] = dot(late_t[at, :], v_sum)
     returned[own * cap:(own + 1) * cap, :] = summed[own * cap:(own + 1) * cap, :]
 
     squares = jnp.zeros((1, 1), F32)
@@ -290,7 +243,6 @@
             total = gram_part[at, other].astype(F32)
             for p in range(1, ndp):
                 total = total + gram_got[p - 1, at, other].astype(F32)
-            total = total + gram_sum[at, other] + gram_sum[other, at].T
             gram_sum[at, other] = total
             here = jnp.sum(jnp.sum(total * total, axis=0, keepdims=True), axis=1, keepdims=True)
             squares = squares + here * (1.0 if i == j else 2.0)
@@ -346,7 +298,6 @@
         for g in range(GROUPS):
             across_scaled(g, p).wait_send()
             across_back(g, p).wait_send()
-        across_v(p).wait_send()
 
 
 def update_kernel(c_ref, p_ref, g_ref, out_ref):
@@ -362,7 +313,6 @@
     capacity = 5 * tokens * top // (4 * n)
     cap = -(-capacity // 16) * 16
     rows = n * cap
-    late = rows // GROUPS
     tiles = hid // min(256, part)
     scaled = (gate_prob[:, :, None] * hidden.astype(F32)).astype(BF16)
     scaled = scaled.transpose(1, 0, 2).reshape(top * tokens, part)
@@ -386,19 +336,16 @@
             pltpu.VMEM((rows, width), BF16),
             pltpu.VMEM((rows, part), BF16),
             pltpu.VMEM((ndp, rows, part), BF16),
-            pltpu.VMEM((hid, rows - late), BF16),
-            pltpu.VMEM((hid, late), BF16),
+            pltpu.VMEM((hid, rows), BF16),
             pltpu.VMEM((ndp, rows, part), BF16),
             pltpu.VMEM((ndp - 1, rows, part), BF16),
             pltpu.VMEM((rows, part), BF16),
             pltpu.VMEM((rows, part), BF16),
             pltpu.VMEM((hid, hid), BF16),
             pltpu.VMEM((ndp - 1, hid, hid), BF16),
-            pltpu.VMEM((late, hid), BF16),
-            pltpu.VMEM((ndp - 1, late, hid), BF16),
             pltpu.VMEM((hid, hid), F32),
             pltpu.VMEM((hid, hid), BF16),
-        ] + [dma((n,))] * 6 + [dma((ndp, GROUPS))] * 4 + [dma((ndp, tiles))] * 2 + [dma((ndp,))] * 2,
+        ] + [dma((n,))] * 6 + [dma((ndp, GROUPS))] * 4 + [dma((ndp, tiles))] * 2,
         compiler_params=pltpu.CompilerParams(
             collective_id=0, has_side_effects=True, vmem_limit_bytes=62 * 1024 * 1024
         ),

time: 231 us -> 244 us (1.056)
  the two profiles are of different devices: /device:TPU:11 before, /device:TPU:1 now
where the time goes in v5:
time: 244 us
  Pallas kernels  233 us (95%)
  local copies, waits for them, and re-layouts  7.58 us (3%)
    pallas_call x1, Pallas kernels, per_device(): pl.pallas_call(functools.partial(kernel, n, ndp, cap), out_shape=[jax.Sha...  225 us
    pallas_call x1, Pallas kernels, per_device(): pl.pallas_call(update_kernel, grid=(width // chunk,), out_shape=jax.Shape...  7.86 us
    unnamed x10, local copies, waits for them, and re-layouts  6.45 us

profile of v5, /device:TPU:1, one launch (start us, length us, event | category | flops | bytes accessed | tf_op | source)
XLA Modules:
  0.0 243.6 jit_solution(5378694643624458556)
XLA Ops:
  0.6 0.8 copy.9.prob_ref
  1.5 0.0 copy-start.3
  1.5 2.2 fusion
  3.6 1.1 copy.8
  4.8 0.0 copy-done.3
  4.8 225.3 %shard_map.68 = (bf16[1024,2048]{1,0:T(8,128)(2,1)}, bf16[1024,1024]{1,0:T(8,128)(2,1)}, f32[8,128]{1,0:T(8,128)}, bf16[2,512,512]{2,1,0:T(8,128)(2,1)}) custom-call(s32[2,512]{1,0:T(2,128)} %bitcast.10, f32[512,2]{1,0:T(8,128)} %copy-done.3, bf16[512,2048]{1,0:T(8,128)(2,1)} %grad_ref.1, bf16[1024,512]{1,0:T(8,128)(2,1)} %bitcast.7, bf16[1024,2048]{1,0:T(8,128)(2,1)} %bitcast.9), custom_call_target="tpu_custom_call" | custom-call | flops 20000000000 | bytes 16000000 | tf_op jit(solution)/shard_map/pallas_call | solution.py:321
  230.1 0.0 copy-start.1
  230.1 0.0 copy-start.2
  230.1 3.4 %copy.10 = bf16[512,2,512]{2,1,0:T(2,128)(2,1)} copy(bf16[512,2,512]{2,0,1:T(8,128)(2,1)} %bitcast.8) | data formatting | bytes 2097152
  233.5 0.0 copy-done.1
  233.5 0.0 copy-done.2
  233.5 0.0 copy-start
  233.5 2.2 copy-done
  235.7 7.9 %shard_map.69 = f32[1024,2048]{1,0:T(8,128)} custom-call(f32[8,128]{1,0:T(8,128)S(1)} %copy-done.2, bf16[1024,1024]{1,0:T(8,128)(2,1)S(1)} %copy-done.1, bf16[1024,2048]{1,0:T(8,128)(2,1)S(1)} %copy-done), custom_call_target="tpu_custom_call" | custom-call | flops 4294967296 | bytes 12582912 | tf_op jit(solution)/shard_map/pallas_call | solution.py:355
Async XLA Ops:
  1.5 3.3 %copy-start.3 = (f32[512,2]{1,0:T(8,128)}, f32[512,2]{1,0:T(8,128)S(1)}, u32[]{:S(2)}) copy-start(f32[512,2]{1,0:T(8,128)S(1)} %copy.9.prob_ref) | copy-start | bytes 12292
  230.1 3.4 %copy-start.1 = (bf16[1024,1024]{1,0:T(8,128)(2,1)S(1)}, bf16[1024,1024]{1,0:T(8,128)(2,1)}, u32[]{:S(2)}) copy-start(bf16[1024,1024]{1,0:T(8,128)(2,1)} %get-tuple-element.8.p_ref) | copy-start | bytes 6291460
  230.1 3.4 %copy-start.2 = (f32[8,128]{1,0:T(8,128)S(1)}, f32[8,128]{1,0:T(8,128)}, u32[]{:S(2)}) copy-start(f32[8,128]{1,0:T(8,128)} %get-tuple-element.7.c_ref) | copy-start | bytes 12292
  233.5 2.2 copy-start
